TPU v7x, 32 devices: a whole 2x2x4 slice. The times are simulated.
32 devices in a mesh: tmpl: 32 (over z, y, x, core), dom: 1.
Axes of the slice: x: 2, y: 2, z: 4, core: 2. Of those that a mesh axis runs over, the one named last changes fastest.
Arguments:
- particles: bfloat16 [4096, 16384], P('tmpl', 'dom'), may hold values from -8 to 8
- templates: bfloat16 [128, 18, 16384], P('tmpl', None, 'dom')
- classes: int32 [4096, 1], P('tmpl'), may hold values from 0 to 127; in each aligned block of 128 rows (0 to 127, 128 to 255, ...) at most 2 rows name the same one
- rotations: int32 [4096], P('tmpl'), may hold values from 0 to 17
Outputs:
- class_means: float32 [128, 18, 16384], P('tmpl', None, 'dom')
- weights: bfloat16 [4096], P('tmpl')
Inputs may be any that keep to these rules, and one draw needn't show every extreme that they name: `classes`: among the 128 particles of one index of tmpl (aligned blocks of rows) no class appears more than 2 times, and some class appears exactly 2 times.
All inputs are finite; a program needn't handle non-finite values.
Results may differ from a plain program's by a relative error of at most 0.0022.
Values may be sent and summed in bfloat16 or wider, within the bound.
A program may use at most 256 MiB of HBM per device.

v0:
```python
import functools

import jax
import jax.numpy as jnp
from jax import lax
from jax.experimental import pallas as pl
from jax.experimental.pallas import tpu as pltpu
from jax.sharding import PartitionSpec as P

CHUNKS = 4
VIA_SPAN = 1
WIDTH = 1024

eps = 1e-05


def place(n):
    me = lax.axis_index("tmpl")
    core = lax.rem(me, 2)
    x = lax.rem(me // 2, 2)
    y = lax.rem(me // 4, 2)
    low = lax.rem(me // 8, 2)
    high = me // 16
    return high, low, y, x, core


def index_of(high, low, y, x, core):
    return (((high * 2 + low) * 2 + y) * 2 + x) * 2 + core


def gather_kernel(n, part_ref, temp_ref, label_ref, parts_ref, sibs_ref, temps_ref, labels_ref, own_sem, ps_sem, pr_sem, ts_sem, tr_sem, ls_sem, lr_sem):
    highs = n // 16
    high, low, y, x, core = place(n)
    pix = part_ref.shape[1]
    width = pix // CHUNKS

    def dev(a, b, c, d, e):
        return {"tmpl": index_of(a, b, c, d, e)}

    to_low = dev(high, 1 - low, y, x, core)
    to_x = dev(high, low, y, 1 - x, core)
    to_diag = dev(high, 1 - low, y, 1 - x, core)
    to_y = dev(high, low, 1 - y, x, core)
    to_core = dev(high, low, y, x, 1 - core)
    others = [lax.rem(high + step, highs) for step in range(1, highs)]
    to_high = [dev(o, low, y, x, core) for o in others]
    came_high = [lax.rem(high + highs - step, highs) for step in range(1, highs)]

    barrier = pltpu.get_barrier_semaphore()
    peers = [to_low, to_x, to_diag, to_y, to_core] + to_high
    for peer in peers:
        pl.semaphore_signal(barrier, inc=1, device_id=peer, device_id_type=pl.DeviceIdType.MESH)
    pl.semaphore_wait(barrier, len(peers))

    def cols(j):
        return pl.ds(j * width, width)

    def send(src, dst, s_sem, r_sem, peer):
        return pltpu.make_async_remote_copy(
            src_ref=src, dst_ref=dst, send_sem=s_sem, recv_sem=r_sem,
            device_id=peer, device_id_type=pl.DeviceIdType.MESH,
        )

    def part(b, d, j):
        return parts_ref.at[b, d, :, cols(j)]

    def temp(a, c, e, j):
        return temps_ref.at[a, c, e, :, cols(j)]

    y0 = highs - 1
    c0 = y0 + highs
    sent = []

    def t_send(kind, src, slot, j, peer):
        cp = send(src, temp(*slot, j), ts_sem.at[kind, j], tr_sem.at[kind, j], peer)
        cp.start()
        sent.append(cp)

    def t_wait(kind, slot, j, peer):
        send(temp(*slot, j), temp(*slot, j), ts_sem.at[kind, j], tr_sem.at[kind, j], peer).wait_recv()

    def p_send(kind, src, slot, j, peer):
        cp = send(src, part(*slot, j), ps_sem.at[kind, j], pr_sem.at[kind, j], peer)
        cp.start()
        sent.append(cp)

    def p_share(i, src, slot, j):
        there = sibs_ref.at[slot[0], slot[1], :, cols(j)]
        cp = send(src, there, ps_sem.at[3 + i, j], pr_sem.at[3 + i, j], to_core)
        cp.start()
        sent.append(cp)

    def p_wait(kind, slot, j, peer):
        send(part(*slot, j), part(*slot, j), ps_sem.at[kind, j], pr_sem.at[kind, j], peer).wait_recv()

    spot = labels_ref.at[low * 2 + x]
    for i, peer in enumerate((to_low, to_x, to_diag)):
        cp = send(label_ref, spot, ls_sem.at[i], lr_sem.at[i], peer)
        cp.start()
        sent.append(cp)
    for j in range(CHUNKS):
        own_t = temp_ref.at[:, cols(j)]
        own_p = part_ref.at[:, cols(j)]
        for i in range(highs - 1):
            t_send(i, own_t, (high, y, core), j, to_high[i])
        p_send(0, own_p, (low, x), j, to_low)
        p_send(1, own_p, (low, x), j, to_x)
        p_share(0, own_p, (low, x), j)
        t_send(y0, own_t, (high, y, core), j, to_y)
        t_send(c0, own_t, (high, y, core), j, to_core)
    own = [
        pltpu.make_async_copy(part_ref, parts_ref.at[low, x], own_sem.at[0]),
        pltpu.make_async_copy(temp_ref, temps_ref.at[high, y, core], own_sem.at[1]),
        pltpu.make_async_copy(label_ref, spot, own_sem.at[2]),
    ]
    for cp in own:
        cp.start()

    for j in range(CHUNKS):
        for i in range(highs - 1):
            slot = (came_high[i], y, core)
            t_wait(i, slot, j, to_high[i])
            t_send(y0 + 1 + i, temp(*slot, j), slot, j, to_y)
            t_send(c0 + 1 + i, temp(*slot, j), slot, j, to_core)
        p_wait(0, (1 - low, x), j, to_low)
        p_share(1, part(1 - low, x, j), (1 - low, x), j)
        if j >= VIA_SPAN:
            p_send(2, part(1 - low, x, j), (1 - low, x), j, to_x)
        p_wait(1, (low, 1 - x), j, to_x)
        p_share(2, part(low, 1 - x, j), (low, 1 - x), j)
        if j < VIA_SPAN:
            p_send(2, part(low, 1 - x, j), (low, 1 - x), j, to_low)
        slot = (high, 1 - y, core)
        t_wait(y0, slot, j, to_y)
        t_send(c0 + highs, temp(*slot, j), slot, j, to_core)
    for j in range(CHUNKS):
        for i in range(highs - 1):
            slot = (came_high[i], 1 - y, core)
            t_wait(y0 + 1 + i, slot, j, to_y)
            t_send(c0 + highs + 1 + i, temp(*slot, j), slot, j, to_core)
    for j in range(CHUNKS):
        p_wait(2, (1 - low, 1 - x), j, to_low if j < VIA_SPAN else to_x)
        p_share(3, part(1 - low, 1 - x, j), (1 - low, 1 - x), j)
        for half in range(2):
            row = y if half == 0 else 1 - y
            t_wait(c0 + half * highs, (high, row, 1 - core), j, to_core)
            for i in range(highs - 1):
                t_wait(c0 + half * highs + 1 + i, (came_high[i], row, 1 - core), j, to_core)
    for i, at in enumerate(((low, x), (1 - low, x), (low, 1 - x), (1 - low, 1 - x))):
        for j in range(CHUNKS):
            there = sibs_ref.at[at[0], at[1], :, cols(j)]
            send(there, there, ps_sem.at[3 + i, j], pr_sem.at[3 + i, j], to_core).wait_recv()
    for i, (b, d) in enumerate(((1 - low, x), (low, 1 - x), (1 - low, 1 - x))):
        there = labels_ref.at[b * 2 + d]
        send(there, there, ls_sem.at[i], lr_sem.at[i], to_low).wait_recv()
    for cp in own:
        cp.wait()
    for cp in sent:
        cp.wait_send()


def gather_blocks(n, particles, flat_templates, label):
    highs = n // 16
    rows, pix = particles.shape
    bins = flat_templates.shape[0]
    kinds = 3 * highs - 1 + highs
    total = (rows * 4 + bins * 4 * highs) * pix * 2
    return pl.pallas_call(
        functools.partial(gather_kernel, n),
        out_shape=(
            jax.ShapeDtypeStruct((2, 2, rows, pix), jnp.bfloat16),
            jax.ShapeDtypeStruct((2, 2, rows, pix), jnp.bfloat16),
            jax.ShapeDtypeStruct((highs, 2, 2, bins, pix), jnp.bfloat16),
            jax.ShapeDtypeStruct((4,) + label.shape, label.dtype),
        ),
        in_specs=[pl.BlockSpec(memory_space=pl.ANY)] * 3,
        out_specs=[pl.BlockSpec(memory_space=pl.ANY)] * 4,
        scratch_shapes=[
            pltpu.SemaphoreType.DMA((3,)),
            pltpu.SemaphoreType.DMA((7, CHUNKS)),
            pltpu.SemaphoreType.DMA((7, CHUNKS)),
            pltpu.SemaphoreType.DMA((kinds, CHUNKS)),
            pltpu.SemaphoreType.DMA((kinds, CHUNKS)),
            pltpu.SemaphoreType.DMA((3,)),
            pltpu.SemaphoreType.DMA((3,)),
        ],
        compiler_params=pltpu.CompilerParams(collective_id=0, has_side_effects=True),
        cost_estimate=pl.CostEstimate(flops=0, bytes_accessed=10 * total, transcendentals=0),
    )(particles, flat_templates, label)


def weigh_kernel(n, columns, both_ref, info_ref, held, as_sem, ar_sem, bs_sem, br_sem):
    highs = n // 16
    high, low, y, x, core = place(n)

    def dev(a, b, c, d, e):
        return {"tmpl": index_of(a, b, c, d, e)}

    near = [(b, d) for b in range(2) for d in range(2) if b or d]
    far = [(a, c, e) for a in range(highs) for c in range(2) for e in range(2) if a or c or e]

    def flip(bit, by):
        return 1 - bit if by else bit

    near_at = [(flip(low, b), flip(x, d)) for b, d in near]
    near_to = [dev(high, b, y, d, core) for b, d in near_at]
    far_to = [dev(lax.rem(high + a, highs), low, flip(y, c), x, flip(core, e)) for a, c, e in far]
    far_at = [(lax.rem(high + highs - a, highs), flip(y, c), flip(core, e)) for a, c, e in far]

    barrier = pltpu.get_barrier_semaphore()
    for peer in near_to + far_to:
        pl.semaphore_signal(barrier, inc=1, device_id=peer, device_id_type=pl.DeviceIdType.MESH)
    pl.semaphore_wait(barrier, len(near_to + far_to))

    def send(src, dst, s_sem, r_sem, peer):
        return pltpu.make_async_remote_copy(
            src_ref=src, dst_ref=dst, send_sem=s_sem, recv_sem=r_sem,
            device_id=peer, device_id_type=pl.DeviceIdType.MESH,
        )

    mine = low * 2 + x
    sent = []
    for i, peer in enumerate(near_to):
        cp = send(both_ref, held.at[mine], as_sem.at[i], ar_sem.at[i], peer)
        cp.start()
        sent.append(cp)
    held[mine] = both_ref[...]
    for i, (b, d) in enumerate(near_at):
        spot = held.at[b * 2 + d]
        send(spot, spot, as_sem.at[i], ar_sem.at[i], near_to[i]).wait_recv()
    total = (held[0] + held[1]) + (held[2] + held[3])
    picked, square = total[:, 0:1], total[:, 1:2]
    weight = (picked * picked / (square / columns + eps)).astype(jnp.bfloat16).astype(jnp.float32)
    row = lax.broadcasted_iota(jnp.int32, total.shape, 1)
    info_ref[high, y, core] = jnp.where(row == 0, weight, both_ref[...])
    own = info_ref.at[high, y, core]
    for i, peer in enumerate(far_to):
        cp = send(own, own, bs_sem.at[i], br_sem.at[i], peer)
        cp.start()
        sent.append(cp)
    for i, at in enumerate(far_at):
        spot = info_ref.at[at[0], at[1], at[2]]
        send(spot, spot, bs_sem.at[i], br_sem.at[i], far_to[i]).wait_recv()
    for cp in sent:
        cp.wait_send()


def weigh_blocks(n, columns, both):
    highs = n // 16
    return pl.pallas_call(
        functools.partial(weigh_kernel, n, columns),
        out_shape=jax.ShapeDtypeStruct((highs, 2, 2) + both.shape, jnp.float32),
        in_specs=[pl.BlockSpec(memory_space=pltpu.VMEM)],
        out_specs=pl.BlockSpec(memory_space=pltpu.VMEM),
        scratch_shapes=[
            pltpu.VMEM((4,) + both.shape, jnp.float32),
            pltpu.SemaphoreType.DMA((3,)),
            pltpu.SemaphoreType.DMA((3,)),
            pltpu.SemaphoreType.DMA((4 * highs - 1,)),
            pltpu.SemaphoreType.DMA((4 * highs - 1,)),
        ],
        compiler_params=pltpu.CompilerParams(collective_id=1, has_side_effects=True),
        cost_estimate=pl.CostEstimate(flops=0, bytes_accessed=20000000, transcendentals=0),
    )(both)


def sum_kernel(n, mix_ref, least_ref, parts_ref, sibs_ref, out_ref, buf, y_out, y_in, kept, h_out, h_in,
               buf_sem, ys_sem, yr_sem, hs_sem, hr_sem):
    highs = n // 16
    high, low, y, x, core = place(n)
    bins = out_ref.shape[0]
    span = highs * bins
    rows = parts_ref.shape[0]
    steps = out_ref.shape[1] // WIDTH

    def dev(a, c):
        return {"tmpl": index_of(a, low, c, x, core)}

    to_y = dev(high, 1 - y)
    to_high = [dev(lax.rem(high + k, highs), y) for k in range(1, highs)]

    barrier = pltpu.get_barrier_semaphore()
    for peer in [to_y] + to_high:
        pl.semaphore_signal(barrier, inc=1, device_id=peer, device_id_type=pl.DeviceIdType.MESH)
    pl.semaphore_wait(barrier, highs)

    def load(j, slot):
        at = pl.ds(pl.multiple_of(j * WIDTH, WIDTH), WIDTH)
        return (
            pltpu.make_async_copy(parts_ref.at[:, at], buf.at[slot, 0], buf_sem.at[slot, 0]),
            pltpu.make_async_copy(sibs_ref.at[:, at], buf.at[slot, 1], buf_sem.at[slot, 1]),
        )

    def send_y(j):
        return pltpu.make_async_remote_copy(
            src_ref=y_out.at[j], dst_ref=y_in.at[j], send_sem=ys_sem.at[j], recv_sem=yr_sem.at[j],
            device_id=to_y, device_id_type=pl.DeviceIdType.MESH,
        )

    def send_h(j, k):
        return pltpu.make_async_remote_copy(
            src_ref=h_out.at[j, k - 1], dst_ref=h_in.at[j, k - 1],
            send_sem=hs_sem.at[j, k - 1], recv_sem=hr_sem.at[j, k - 1],
            device_id=to_high[k - 1], device_id_type=pl.DeviceIdType.MESH,
        )

    for cp in load(0, 0):
        cp.start()

    def form(j, carry):
        slot = lax.rem(j, 2)

        @pl.when(j + 1 < steps)
        def _():
            for cp in load(j + 1, 1 - slot):
                cp.start()

        for cp in load(j, slot):
            cp.wait()
        mix = mix_ref[...]
        both = jnp.dot(mix[:, :rows], buf[slot, 0], preferred_element_type=jnp.float32)
        both += jnp.dot(mix[:, rows:], buf[slot, 1], preferred_element_type=jnp.float32)
        y_out[j] = both[:span].astype(jnp.bfloat16)
        kept[j] = both[span:]
        send_y(j).start()
        return carry

    def merge(j, carry):
        send_y(j).wait_recv()
        total = kept[j] + y_in[j].astype(jnp.float32)
        kept[j] = total
        for k in range(1, highs):
            h_out[j, k - 1] = total[k * bins:(k + 1) * bins].astype(jnp.bfloat16)
            send_h(j, k).start()
        return carry

    def finish(j, carry):
        total = kept[j][:bins]
        for k in range(1, highs):
            send_h(j, k).wait_recv()
            total += h_in[j, k - 1].astype(jnp.float32)
        out_ref[:, pl.ds(pl.multiple_of(j * WIDTH, WIDTH), WIDTH)] = total / least_ref[:, 0:1]
        return carry

    def drain(j, carry):
        send_y(j).wait_send()
        for k in range(1, highs):
            send_h(j, k).wait_send()
        return carry

    for stage in (form, merge, finish, drain):
        lax.fori_loop(0, steps, stage, 0)


def sum_blocks(n, mix, least, parts, sibs):
    highs = n // 16
    rows, pix = parts.shape
    bins = least.shape[0]
    steps = pix // WIDTH
    anywhere = pl.BlockSpec(memory_space=pl.ANY)
    local = pl.BlockSpec(memory_space=pltpu.VMEM)
    return pl.pallas_call(
        functools.partial(sum_kernel, n),
        out_shape=jax.ShapeDtypeStruct((bins, pix), jnp.float32),
        in_specs=[local, local, anywhere, anywhere],
        out_specs=local,
        scratch_shapes=[
            pltpu.VMEM((2, 2, rows, WIDTH), jnp.bfloat16),
            pltpu.VMEM((steps, highs * bins, WIDTH), jnp.bfloat16),
            pltpu.VMEM((steps, highs * bins, WIDTH), jnp.bfloat16),
            pltpu.VMEM((steps, highs * bins, WIDTH), jnp.float32),
            pltpu.VMEM((steps, highs - 1, bins, WIDTH), jnp.bfloat16),
            pltpu.VMEM((steps, highs - 1, bins, WIDTH), jnp.bfloat16),
            pltpu.SemaphoreType.DMA((2, 2)),
            pltpu.SemaphoreType.DMA((steps,)),
            pltpu.SemaphoreType.DMA((steps,)),
            pltpu.SemaphoreType.DMA((steps, highs - 1)),
            pltpu.SemaphoreType.DMA((steps, highs - 1)),
        ],
        compiler_params=pltpu.CompilerParams(
            collective_id=2, has_side_effects=True, vmem_limit_bytes=48 * 1024 * 1024
        ),
        cost_estimate=pl.CostEstimate(
            flops=4 * rows * mix.shape[0] * pix, bytes_accessed=4 * rows * pix, transcendentals=0
        ),
    )(mix, least, parts, sibs)


def body(particles, templates, classes, rotations):
    rows, pix = particles.shape
    local_classes, rot_count, _ = templates.shape
    n = lax.axis_size("tmpl")
    highs = n // 16
    bins = local_classes * rot_count
    total_bins = bins * n
    high, low, y, x, core = place(n)
    me = lax.axis_index("tmpl")

    class_ids = classes[:, 0]
    target = class_ids // local_classes * bins + rotations * local_classes + class_ids % local_classes
    label = jnp.pad(target[None], ((2, 5), (0, 0)))
    flat = templates.transpose(1, 0, 2).reshape(bins, pix)
    parts, sibs, temps, labels = gather_blocks(n, particles, flat, label)
    parts = parts.reshape(4 * rows, pix)
    sibs = sibs.reshape(4 * rows, pix)
    temps = temps.reshape(4 * highs * bins, pix)
    scores = lax.dot_general(parts, temps, (((1,), (1,)), ((), ())), preferred_element_type=jnp.float32)
    if lax.axis_size("dom") > 1:
        scores = lax.psum(scores, "dom")

    shape = (highs, 2, 2, bins)
    owner, o_y, o_c, o_b = [lax.broadcasted_iota(jnp.int32, shape, i) for i in range(4)]
    column = (index_of(owner, low, o_y, x, o_c) * bins + o_b).reshape(1, 4 * highs * bins)
    near = labels[:, 2].reshape(4 * rows)
    picked = jnp.sum(jnp.where(column == near[:, None], scores, 0.0), axis=1)
    square = jnp.sum(scores * scores, axis=1)
    both = jnp.stack([picked.reshape(4, rows), square.reshape(4, rows)], axis=1)
    both = jnp.pad(both, ((0, 0), (0, 6), (0, 0))) + labels.astype(jnp.float32)
    info = weigh_blocks(n, float(total_bins), both)

    def rows_of(e):
        block = lax.dynamic_slice(info, (high, y, e, 0, 0, 0), (1, 1, 1, 4, 8, rows))
        return block.reshape(4, 8, rows)

    here = rows_of(core)
    weights = lax.dynamic_index_in_dim(here, low * 2 + x, 0, keepdims=False)[0].astype(jnp.bfloat16)
    chip = jnp.stack([here, rows_of(1 - core)])
    chip_w = chip[:, :, 0].reshape(1, 8 * rows)
    chip_t = chip[:, :, 2].astype(jnp.int32).reshape(1, 8 * rows)
    shape = (2, highs, bins)
    flip, ahead, o_b = [lax.broadcasted_iota(jnp.int32, shape, i) for i in range(3)]
    o_y = jnp.where(flip == 0, 1 - y, y)
    wanted = index_of((high + ahead) % highs, low, o_y, x, core) * bins + o_b
    mix = jnp.where(wanted.reshape(2 * highs * bins, 1) == chip_t, chip_w, 0.0).astype(jnp.bfloat16)

    all_w = info[..., 0, :].reshape(1, n * rows)
    all_t = info[..., 2, :].astype(jnp.int32).reshape(1, n * rows)
    own = me * bins + lax.broadcasted_iota(jnp.int32, (bins, 1), 0)
    totals = jnp.sum(jnp.where(own == all_t, all_w, 0.0), axis=1)
    least = jnp.broadcast_to(jnp.maximum(totals, 1.0)[:, None], (bins, 128))
    means = sum_blocks(n, mix, least, parts, sibs)
    return means.reshape(rot_count, local_classes, pix).transpose(1, 0, 2), weights


def solution(mesh):
    return jax.shard_map(
        body,
        mesh=mesh,
        in_specs=(P("tmpl", "dom"), P("tmpl", None, "dom"), P("tmpl", None), P("tmpl")),
        out_specs=(P("tmpl", None, "dom"), P("tmpl")),
        check_vma=False,
    )
```

profile of v0, /device:TPU:0, one launch (start us, length us, event | category | flops | bytes accessed | tf_op | source)
XLA Modules:
  0.0 382.5 jit_solution(10852432092612348928)
XLA Ops:
  0.6 0.0 copy-start.2
  0.6 0.0 copy-start.3
  0.7 5.0 %reshape.141.temp_ref = bf16[72,16384]{1,0:T(8,128)(2,1)} reshape(bf16[18,4,16384]{2,1,0:T(4,128)(2,1)} %bitcast.41) | data formatting | bytes 4718592 | tf_op jit(solution)/shard_map/reshape | solution.py:402
  5.6 0.0 copy-done.2
  5.6 0.0 copy-done.3
  5.7 0.6 pad.8.label_ref
  6.3 205.0 %shard_map.59 = (bf16[2,2,128,16384]{3,2,1,0:T(8,128)(2,1)}, bf16[2,2,128,16384]{3,2,1,0:T(8,128)(2,1)}, bf16[2,2,2,72,16384]{4,3,2,1,0:T(8,128)(2,1)}, s32[4,8,128]{2,1,0:T(8,128)}) custom-call(bf16[128,16384]{1,0:T(8,128)(2,1)} %part_ref.1, bf16[72,16384]{1,0:T(8,128)(2,1)} %reshape.141.temp_ref, s32[8,128]{1,0:T(8,128)} %pad.8.label_ref), custom_call_target="tpu_custom_call" | custom-call | bytes 356515840 | tf_op jit(solution)/shard_map/pallas_call | solution.py:168
  211.3 0.7 slice.20
  212.0 0.1 multiply_add_fusion
  212.1 0.1 reshape.153
  212.2 0.0 copy-start.1
  212.2 18.7 %select_reduce_fusion.1 = (f32[512]{0:T(512)S(1)}, f32[512]{0:T(512)S(1)}) fusion(s32[512]{0:T(512)S(1)} %bitcast.48, s32[576]{0:T(1024)S(1)} %reshape.153, bf16[512,16384]{1,0:T(8,128)(2,1)} %bitcast.37, bf16[576,16384]{1,0:T(8,128)(2,1)} %bitcast.49), kind=kOutput, calls=%fused_computation.3 | convolution fusion | flops 9665150976 | bytes 35660032 | tf_op jit(solution)/shard_map/dot_general | solution.py:407
  230.9 0.0 copy-done.1
  230.9 0.6 fusion.both_ref
  231.5 12.6 %shard_map.60 = f32[2,2,2,4,8,128]{5,4,3,2,1,0:T(8,128)} custom-call(f32[4,8,128]{2,1,0:T(8,128)} %fusion.both_ref), custom_call_target="tpu_custom_call" | custom-call | bytes 20000000 | tf_op jit(solution)/shard_map/pallas_call | solution.py:250
  244.2 0.7 dynamic-slice_bitcast_fusion.1
  245.0 0.1 iota.66
  245.0 0.1 iota.64
  245.1 0.1 select_n.90
  245.2 0.1 iota.61
  245.3 0.1 iota.62
  245.4 0.2 select_convert_fusion.mix_ref
  245.6 1.0 slice_convert_fusion
  246.6 0.3 select_reduce_fusion
  246.9 0.1 broadcast_in_dim.59.least_ref
  247.0 125.9 %shard_map.61 = f32[72,16384]{1,0:T(8,128)S(1)} custom-call(bf16[288,1024]{1,0:T(8,128)(2,1)S(1)} %select_convert_fusion.mix_ref, f32[72,128]{1,0:T(8,128)S(1)} %broadcast_in_dim.59.least_ref, bf16[512,16384]{1,0:T(8,128)(2,1)} %bitcast.38, bf16[512,16384]{1,0:T(8,128)(2,1)} %bitcast.39), custom_call_target="tpu_custom_call" | custom-call | flops 9663676416 | bytes 33554432 | tf_op jit(solution)/shard_map/pallas_call | solution.py:362
  372.9 0.0 copy-start
  372.9 2.1 copy-done
  375.0 6.3 %reshape.145 = f32[18,4,16384]{2,1,0:T(4,128)} reshape(f32[72,16384]{1,0:T(8,128)} %copy-done) | data formatting | bytes 9437184 | tf_op jit(solution)/shard_map/reshape | solution.py:442
  381.3 0.7 dynamic-slice_convert_fusion
  382.0 0.5 slice_bitcast_fusion
  (9 shorter events, 0.1 us)
Async XLA Ops:
  0.6 5.0 %copy-start.2 = (s32[128]{0:T(128)S(1)}, s32[128]{0:T(128)}, u32[]{:S(2)}) copy-start(s32[128]{0:T(128)} %param.7) | copy-start | bytes 1540
  0.6 5.0 %copy-start.3 = (s32[128,1]{0,1:T(1,128)S(1)}, s32[128,1]{0,1:T(1,128)}, u32[]{:S(2)}) copy-start(s32[128,1]{0,1:T(1,128)} %param.6) | copy-start | bytes 1540
  212.2 18.7 %copy-start.1 = (s32[4,8,128]{2,1,0:T(8,128)S(1)}, s32[4,8,128]{2,1,0:T(8,128)}, u32[]{:S(2)}) copy-start(s32[4,8,128]{2,1,0:T(8,128)} %get-tuple-element.6) | copy-start | bytes 49156
  372.9 2.1 copy-start
where the time goes:
time: 383 us; the launch traced here: 382 us
  Pallas kernels  344 us (90%)
  matrix products  18.7 us (5%)
  local copies, waits for them, and re-layouts  17.2 us (4%)
    pallas_call x1, Pallas kernels, gather_blocks(): pl.pallas_call(functools.partial(gather_kernel, n), out_shape=(jax.ShapeD...  205 us
    pallas_call x1, Pallas kernels, sum_blocks(): pl.pallas_call(functools.partial(sum_kernel, n), out_shape=jax.ShapeDtype...  126 us
    dot_general x1, matrix products, body(): lax.dot_general(parts, temps, (((1,), (1,)), ((), ())), preferred_element...  18.7 us
    pallas_call x1, Pallas kernels, weigh_blocks(): pl.pallas_call(functools.partial(weigh_kernel, n, columns), out_shape=jax...  12.6 us

commit v1 on v0

--- a/solution.py
+++ b/solution.py
@@ -7,8 +7,8 @@
 from jax.experimental.pallas import tpu as pltpu
 from jax.sharding import PartitionSpec as P
 
-CHUNKS = 4
-VIA_SPAN = 1
+CHUNKS = 8
+VIA_SPAN = 2
 WIDTH = 1024
 
 eps = 1e-05
@@ -28,7 +28,7 @@
     return (((high * 2 + low) * 2 + y) * 2 + x) * 2 + core
 
 
-def gather_kernel(n, part_ref, temp_ref, label_ref, parts_ref, sibs_ref, temps_ref, labels_ref, own_sem, ps_sem, pr_sem, ts_sem, tr_sem, ls_sem, lr_sem):
+def gather_kernel(n, part_ref, temp_ref, label_ref, parts_ref, sibs_ref, temps_ref, labels_ref, score_ref, p_buf, t_buf, buf_sem, own_sem, ps_sem, pr_sem, ts_sem, tr_sem, ls_sem, lr_sem):
     highs = n // 16
     high, low, y, x, core = place(n)
     pix = part_ref.shape[1]
@@ -116,36 +116,66 @@
     for cp in own:
         cp.start()
 
-    for j in range(CHUNKS):
+    def first_hop(j):
         for i in range(highs - 1):
             slot = (came_high[i], y, core)
             t_wait(i, slot, j, to_high[i])
             t_send(y0 + 1 + i, temp(*slot, j), slot, j, to_y)
             t_send(c0 + 1 + i, temp(*slot, j), slot, j, to_core)
         p_wait(0, (1 - low, x), j, to_low)
-        p_share(1, part(1 - low, x, j), (1 - low, x), j)
         if j >= VIA_SPAN:
             p_send(2, part(1 - low, x, j), (1 - low, x), j, to_x)
+        p_share(1, part(1 - low, x, j), (1 - low, x), j)
         p_wait(1, (low, 1 - x), j, to_x)
-        p_share(2, part(low, 1 - x, j), (low, 1 - x), j)
         if j < VIA_SPAN:
             p_send(2, part(low, 1 - x, j), (low, 1 - x), j, to_low)
+        p_share(2, part(low, 1 - x, j), (low, 1 - x), j)
         slot = (high, 1 - y, core)
         t_wait(y0, slot, j, to_y)
         t_send(c0 + highs, temp(*slot, j), slot, j, to_core)
-    for j in range(CHUNKS):
+
+    def second_hop(j):
         for i in range(highs - 1):
             slot = (came_high[i], 1 - y, core)
             t_wait(y0 + 1 + i, slot, j, to_y)
             t_send(c0 + highs + 1 + i, temp(*slot, j), slot, j, to_core)
-    for j in range(CHUNKS):
         p_wait(2, (1 - low, 1 - x), j, to_low if j < VIA_SPAN else to_x)
         p_share(3, part(1 - low, 1 - x, j), (1 - low, 1 - x), j)
+
+    def loads(j):
+        return (
+            pltpu.make_async_copy(parts_ref.at[:, :, :, cols(j)], p_buf.at[j % 2], buf_sem.at[j % 2, 0]),
+            pltpu.make_async_copy(temps_ref.at[:, :, :, :, cols(j)], t_buf.at[j % 2], buf_sem.at[j % 2, 1]),
+        )
+
+    def third_hop(j):
         for half in range(2):
             row = y if half == 0 else 1 - y
             t_wait(c0 + half * highs, (high, row, 1 - core), j, to_core)
             for i in range(highs - 1):
                 t_wait(c0 + half * highs + 1 + i, (came_high[i], row, 1 - core), j, to_core)
+        if j == 0:
+            own[0].wait()
+            own[1].wait()
+        for cp in loads(j):
+            cp.start()
+
+    def score(j):
+        for cp in loads(j):
+            cp.wait()
+        left = p_buf[j % 2].reshape(4 * part_ref.shape[0], width)
+        slots = [(a, c, e) for a in range(highs) for c in range(2) for e in range(2)]
+        right = jnp.concatenate([t_buf[(j % 2,) + at] for at in slots], axis=0)
+        more = lax.dot_general(left, right, (((1,), (1,)), ((), ())), preferred_element_type=jnp.float32)
+        if j == 0:
+            score_ref[...] = more
+        else:
+            score_ref[...] += more
+
+    for j in range(CHUNKS + 3):
+        for late, stage in enumerate((first_hop, second_hop, third_hop, score)):
+            if 0 <= j - late < CHUNKS:
+                stage(j - late)
     for i, at in enumerate(((low, x), (1 - low, x), (low, 1 - x), (1 - low, 1 - x))):
         for j in range(CHUNKS):
             there = sibs_ref.at[at[0], at[1], :, cols(j)]
@@ -153,8 +183,7 @@
     for i, (b, d) in enumerate(((1 - low, x), (low, 1 - x), (1 - low, 1 - x))):
         there = labels_ref.at[b * 2 + d]
         send(there, there, ls_sem.at[i], lr_sem.at[i], to_low).wait_recv()
-    for cp in own:
-        cp.wait()
+    own[2].wait()
     for cp in sent:
         cp.wait_send()
 
@@ -172,10 +201,14 @@
             jax.ShapeDtypeStruct((2, 2, rows, pix), jnp.bfloat16),
             jax.ShapeDtypeStruct((highs, 2, 2, bins, pix), jnp.bfloat16),
             jax.ShapeDtypeStruct((4,) + label.shape, label.dtype),
+            jax.ShapeDtypeStruct((4 * rows, 4 * highs * bins), jnp.float32),
         ),
         in_specs=[pl.BlockSpec(memory_space=pl.ANY)] * 3,
-        out_specs=[pl.BlockSpec(memory_space=pl.ANY)] * 4,
+        out_specs=[pl.BlockSpec(memory_space=pl.ANY)] * 4 + [pl.BlockSpec(memory_space=pltpu.VMEM)],
         scratch_shapes=[
+            pltpu.VMEM((2, 2, 2, rows, pix // CHUNKS), jnp.bfloat16),
+            pltpu.VMEM((2, highs, 2, 2, bins, pix // CHUNKS), jnp.bfloat16),
+            pltpu.SemaphoreType.DMA((2, 2)),
             pltpu.SemaphoreType.DMA((3,)),
             pltpu.SemaphoreType.DMA((7, CHUNKS)),
             pltpu.SemaphoreType.DMA((7, CHUNKS)),
@@ -184,7 +217,9 @@
             pltpu.SemaphoreType.DMA((3,)),
             pltpu.SemaphoreType.DMA((3,)),
         ],
-        compiler_params=pltpu.CompilerParams(collective_id=0, has_side_effects=True),
+        compiler_params=pltpu.CompilerParams(
+            collective_id=0, has_side_effects=True, vmem_limit_bytes=40 * 1024 * 1024
+        ),
         cost_estimate=pl.CostEstimate(flops=0, bytes_accessed=10 * total, transcendentals=0),
     )(particles, flat_templates, label)
 
@@ -400,11 +435,9 @@
     target = class_ids // local_classes * bins + rotations * local_classes + class_ids % local_classes
     label = jnp.pad(target[None], ((2, 5), (0, 0)))
     flat = templates.transpose(1, 0, 2).reshape(bins, pix)
-    parts, sibs, temps, labels = gather_blocks(n, particles, flat, label)
+    parts, sibs, _, labels, scores = gather_blocks(n, particles, flat, label)
     parts = parts.reshape(4 * rows, pix)
     sibs = sibs.reshape(4 * rows, pix)
-    temps = temps.reshape(4 * highs * bins, pix)
-    scores = lax.dot_general(parts, temps, (((1,), (1,)), ((), ())), preferred_element_type=jnp.float32)
     if lax.axis_size("dom") > 1:
         scores = lax.psum(scores, "dom")
 

time: 383 us -> 397 us (1.037)
  Pallas kernels: 344 us -> 373 us
  matrix products: 18.7 us -> 0 us
    pallas_call x1, Pallas kernels: 205 us -> 237 us  [gather_blocks(): pl.pallas_call(functools.partial(gather_kernel, n), out_shape=(jax.ShapeD...]
    dot_general x1 -> x0, matrix products: 18.7 us -> none  [body(): lax.dot_general(parts, temps, (((1,), (1,)), ((), ())), preferred_element...]
where the time goes in v1:
time: 397 us; the launch traced here: 396 us
  Pallas kernels  373 us (94%)
  local copies, waits for them, and re-layouts  18 us (5%)
    pallas_call x1, Pallas kernels, gather_blocks(): pl.pallas_call(functools.partial(gather_kernel, n), out_shape=(jax.ShapeD...  237 us
    pallas_call x1, Pallas kernels, sum_blocks(): pl.pallas_call(functools.partial(sum_kernel, n), out_shape=jax.ShapeDtype...  126 us
    pallas_call x1, Pallas kernels, weigh_blocks(): pl.pallas_call(functools.partial(weigh_kernel, n, columns), out_shape=jax...  10.1 us

profile of v1, /device:TPU:0, one launch (start us, length us, event | category | flops | bytes accessed | tf_op | source)
XLA Modules:
  0.0 396.0 jit_solution(1496828164935889372)
XLA Ops:
  0.6 0.0 copy-start.3
  0.6 0.0 copy-start.4
  0.7 3.9 reshape.138.temp_ref
  4.5 0.0 copy-done.3
  4.6 0.0 copy-done.4
  4.6 0.0 copy-start.1
  4.6 2.2 copy-done.1
  6.8 236.7 %shard_map.59 = (bf16[2,2,128,16384]{3,2,1,0:T(8,128)(2,1)}, bf16[2,2,128,16384]{3,2,1,0:T(8,128)(2,1)}, bf16[2,2,2,72,16384]{4,3,2,1,0:T(8,128)(2,1)}, s32[4,8,128]{2,1,0:T(8,128)S(1)}, f32[512,576]{1,0:T(8,128)S(1)}) custom-call(bf16[128,16384]{1,0:T(8,128)(2,1)S(1)} %copy-done.1, bf16[72,16384]{1,0:T(8,128)(2,1)S(1)} %reshape.138.temp_ref, ...), custom_call_target="tpu_custom_call" | custom-call | bytes 356515840 | tf_op jit(solution)/shard_map/pallas_call | solution.py:197
  243.5 0.0 copy-start.2
  243.5 1.0 copy-done.2
  244.6 0.1 multiply_add_fusion
  244.7 0.1 reshape.149
  244.8 1.7 select_reduce_fusion
  246.4 0.6 fusion.both_ref
  247.1 10.1 %shard_map.60 = f32[2,2,2,4,8,128]{5,4,3,2,1,0:T(8,128)} custom-call(f32[4,8,128]{2,1,0:T(8,128)} %fusion.both_ref), custom_call_target="tpu_custom_call" | custom-call | bytes 20000000 | tf_op jit(solution)/shard_map/pallas_call | solution.py:285
  257.2 0.7 dynamic-slice_bitcast_fusion.1
  258.0 0.1 iota.66
  258.1 0.1 iota.64
  258.2 0.1 select_n.90
  258.3 0.1 iota.61
  258.3 0.1 iota.62
  258.5 0.2 select_convert_fusion.mix_ref
  258.6 1.0 slice_convert_fusion
  259.7 0.3 select_reduce_fusion.1
  260.0 0.1 broadcast_in_dim.59.least_ref
  260.0 126.4 %shard_map.61 = f32[72,16384]{1,0:T(8,128)S(1)} custom-call(bf16[288,1024]{1,0:T(8,128)(2,1)S(1)} %select_convert_fusion.mix_ref, f32[72,128]{1,0:T(8,128)S(1)} %broadcast_in_dim.59.least_ref, bf16[512,16384]{1,0:T(8,128)(2,1)} %bitcast.34, bf16[512,16384]{1,0:T(8,128)(2,1)} %bitcast.35), custom_call_target="tpu_custom_call" | custom-call | flops 9663676416 | bytes 33554432 | tf_op jit(solution)/shard_map/pallas_call | solution.py:397
  386.4 0.0 copy-start
  386.5 2.1 copy-done
  388.6 6.3 %reshape.141 = f32[18,4,16384]{2,1,0:T(4,128)} reshape(f32[72,16384]{1,0:T(8,128)} %copy-done) | data formatting | bytes 9437184 | tf_op jit(solution)/shard_map/reshape | solution.py:475
  394.8 0.7 dynamic-slice_convert_fusion
  395.5 0.5 slice_bitcast_fusion
  (11 shorter events, 0.1 us)
Async XLA Ops:
  0.6 3.9 copy-start.3
  0.6 3.9 copy-start.4
  4.6 2.2 copy-start.1
  243.5 1.1 copy-start.2
  386.4 2.1 copy-start

commit v2 on v1

--- a/solution.py
+++ b/solution.py
@@ -7,8 +7,8 @@
 from jax.experimental.pallas import tpu as pltpu
 from jax.sharding import PartitionSpec as P
 
-CHUNKS = 8
-VIA_SPAN = 2
+CHUNKS = 4
+VIA_SPAN = 1
 WIDTH = 1024
 
 eps = 1e-05
@@ -103,7 +103,8 @@
         own_p = part_ref.at[:, cols(j)]
         for i in range(highs - 1):
             t_send(i, own_t, (high, y, core), j, to_high[i])
-        p_send(0, own_p, (low, x), j, to_low)
+        k = (j + VIA_SPAN) % CHUNKS
+        p_send(0, part_ref.at[:, cols(k)], (low, x), k, to_low)
         p_send(1, own_p, (low, x), j, to_x)
         p_share(0, own_p, (low, x), j)
         t_send(y0, own_t, (high, y, core), j, to_y)
@@ -122,10 +123,11 @@
             t_wait(i, slot, j, to_high[i])
             t_send(y0 + 1 + i, temp(*slot, j), slot, j, to_y)
             t_send(c0 + 1 + i, temp(*slot, j), slot, j, to_core)
-        p_wait(0, (1 - low, x), j, to_low)
-        if j >= VIA_SPAN:
-            p_send(2, part(1 - low, x, j), (1 - low, x), j, to_x)
-        p_share(1, part(1 - low, x, j), (1 - low, x), j)
+        k = (j + VIA_SPAN) % CHUNKS
+        p_wait(0, (1 - low, x), k, to_low)
+        if k >= VIA_SPAN:
+            p_send(2, part(1 - low, x, k), (1 - low, x), k, to_x)
+        p_share(1, part(1 - low, x, k), (1 - low, x), k)
         p_wait(1, (low, 1 - x), j, to_x)
         if j < VIA_SPAN:
             p_send(2, part(low, 1 - x, j), (low, 1 - x), j, to_low)
@@ -139,13 +141,15 @@
             slot = (came_high[i], 1 - y, core)
             t_wait(y0 + 1 + i, slot, j, to_y)
             t_send(c0 + highs + 1 + i, temp(*slot, j), slot, j, to_core)
+
+    def diagonal(j):
         p_wait(2, (1 - low, 1 - x), j, to_low if j < VIA_SPAN else to_x)
         p_share(3, part(1 - low, 1 - x, j), (1 - low, 1 - x), j)
 
     def loads(j):
         return (
-            pltpu.make_async_copy(parts_ref.at[:, :, :, cols(j)], p_buf.at[j % 2], buf_sem.at[j % 2, 0]),
-            pltpu.make_async_copy(temps_ref.at[:, :, :, :, cols(j)], t_buf.at[j % 2], buf_sem.at[j % 2, 1]),
+            pltpu.make_async_copy(parts_ref.at[:, :, :, cols(j)], p_buf.at[order.index(j) % 2], buf_sem.at[order.index(j) % 2, 0]),
+            pltpu.make_async_copy(temps_ref.at[:, :, :, :, cols(j)], t_buf.at[order.index(j) % 2], buf_sem.at[order.index(j) % 2, 1]),
         )
 
     def third_hop(j):
@@ -154,28 +158,34 @@
             t_wait(c0 + half * highs, (high, row, 1 - core), j, to_core)
             for i in range(highs - 1):
                 t_wait(c0 + half * highs + 1 + i, (came_high[i], row, 1 - core), j, to_core)
-        if j == 0:
-            own[0].wait()
-            own[1].wait()
         for cp in loads(j):
             cp.start()
 
     def score(j):
         for cp in loads(j):
             cp.wait()
-        left = p_buf[j % 2].reshape(4 * part_ref.shape[0], width)
+        left = p_buf[order.index(j) % 2].reshape(4 * part_ref.shape[0], width)
         slots = [(a, c, e) for a in range(highs) for c in range(2) for e in range(2)]
-        right = jnp.concatenate([t_buf[(j % 2,) + at] for at in slots], axis=0)
+        right = jnp.concatenate([t_buf[(order.index(j) % 2,) + at] for at in slots], axis=0)
         more = lax.dot_general(left, right, (((1,), (1,)), ((), ())), preferred_element_type=jnp.float32)
-        if j == 0:
+        if j == order[0]:
             score_ref[...] = more
         else:
             score_ref[...] += more
 
-    for j in range(CHUNKS + 3):
-        for late, stage in enumerate((first_hop, second_hop, third_hop, score)):
-            if 0 <= j - late < CHUNKS:
-                stage(j - late)
+    order = [(j + VIA_SPAN) % CHUNKS for j in range(CHUNKS)]
+    for j in range(CHUNKS):
+        first_hop(j)
+    for j in range(CHUNKS):
+        second_hop(j)
+    own[0].wait()
+    own[1].wait()
+    for step, j in enumerate(order):
+        diagonal(j)
+        third_hop(j)
+        if step:
+            score(order[step - 1])
+    score(order[-1])
     for i, at in enumerate(((low, x), (1 - low, x), (low, 1 - x), (1 - low, 1 - x))):
         for j in range(CHUNKS):
             there = sibs_ref.at[at[0], at[1], :, cols(j)]
@@ -218,7 +228,7 @@
             pltpu.SemaphoreType.DMA((3,)),
         ],
         compiler_params=pltpu.CompilerParams(
-            collective_id=0, has_side_effects=True, vmem_limit_bytes=40 * 1024 * 1024
+            collective_id=0, has_side_effects=True, vmem_limit_bytes=48 * 1024 * 1024
         ),
         cost_estimate=pl.CostEstimate(flops=0, bytes_accessed=10 * total, transcendentals=0),
     )(particles, flat_templates, label)
@@ -303,10 +313,11 @@
                buf_sem, ys_sem, yr_sem, hs_sem, hr_sem):
     highs = n // 16
     high, low, y, x, core = place(n)
-    bins = out_ref.shape[0]
+    rots, owned, pix = out_ref.shape
+    bins = rots * owned
     span = highs * bins
     rows = parts_ref.shape[0]
-    steps = out_ref.shape[1] // WIDTH
+    steps = pix // WIDTH
 
     def dev(a, c):
         return {"tmpl": index_of(a, low, c, x, core)}
@@ -374,7 +385,10 @@
         for k in range(1, highs):
             send_h(j, k).wait_recv()
             total += h_in[j, k - 1].astype(jnp.float32)
-        out_ref[:, pl.ds(pl.multiple_of(j * WIDTH, WIDTH), WIDTH)] = total / least_ref[:, 0:1]
+        means = total / least_ref[:, 0:1]
+        at = pl.ds(pl.multiple_of(j * WIDTH, WIDTH), WIDTH)
+        for r in range(rots):
+            out_ref[r, :, at] = means[r * owned:(r + 1) * owned]
         return carry
 
     def drain(j, carry):
@@ -387,7 +401,7 @@
         lax.fori_loop(0, steps, stage, 0)
 
 
-def sum_blocks(n, mix, least, parts, sibs):
+def sum_blocks(n, rots, mix, least, parts, sibs):
     highs = n // 16
     rows, pix = parts.shape
     bins = least.shape[0]
@@ -396,7 +410,7 @@
     local = pl.BlockSpec(memory_space=pltpu.VMEM)
     return pl.pallas_call(
         functools.partial(sum_kernel, n),
-        out_shape=jax.ShapeDtypeStruct((bins, pix), jnp.float32),
+        out_shape=jax.ShapeDtypeStruct((rots, bins // rots, pix), jnp.float32),
         in_specs=[local, local, anywhere, anywhere],
         out_specs=local,
         scratch_shapes=[
@@ -471,8 +485,8 @@
     own = me * bins + lax.broadcasted_iota(jnp.int32, (bins, 1), 0)
     totals = jnp.sum(jnp.where(own == all_t, all_w, 0.0), axis=1)
     least = jnp.broadcast_to(jnp.maximum(totals, 1.0)[:, None], (bins, 128))
-    means = sum_blocks(n, mix, least, parts, sibs)
-    return means.reshape(rot_count, local_classes, pix).transpose(1, 0, 2), weights
+    means = sum_blocks(n, rot_count, mix, least, parts, sibs)
+    return means.transpose(1, 0, 2), weights
 
 
 def solution(mesh):

time: 397 us -> 335 us (0.84)
  Pallas kernels: 373 us -> 315 us
    pallas_call x1, Pallas kernels: 237 us -> 178 us  [gather_blocks(): pl.pallas_call(functools.partial(gather_kernel, n), out_shape=(jax.ShapeD...]
    reshape x1 -> x0, local copies, waits for them, and re-layouts: 6.26 us -> none  [body(): means.reshape(rot_count, local_classes, pix).transpose(1, 0, 2)]
    unnamed x10 -> x9, local copies, waits for them, and re-layouts: 5.35 us -> 8.1 us
where the time goes in v2:
time: 335 us; the launch traced here: 334 us
  Pallas kernels  315 us (94%)
  local copies, waits for them, and re-layouts  14.5 us (4%)
  other arithmetic  3.93 us (1%)
    pallas_call x1, Pallas kernels, gather_blocks(): pl.pallas_call(functools.partial(gather_kernel, n), out_shape=(jax.ShapeD...  178 us
    pallas_call x1, Pallas kernels, sum_blocks(): pl.pallas_call(functools.partial(sum_kernel, n), out_shape=jax.ShapeDtype...  126 us
    pallas_call x1, Pallas kernels, weigh_blocks(): pl.pallas_call(functools.partial(weigh_kernel, n, columns), out_shape=jax...  11 us
    unnamed x9, local copies, waits for them, and re-layouts  8.1 us

profile of v2, /device:TPU:0, one launch (start us, length us, event | category | flops | bytes accessed | tf_op | source)
XLA Modules:
  0.0 334.0 jit_solution(4341801390006960900)
XLA Ops:
  0.6 0.0 copy-start.2
  0.6 0.0 copy-start.3
  0.7 3.9 %reshape.135.temp_ref = bf16[72,16384]{1,0:T(8,128)(2,1)S(1)} reshape(bf16[18,4,16384]{2,1,0:T(4,128)(2,1)} %bitcast.37) | data formatting | bytes 4718592 | tf_op jit(solution)/shard_map/reshape | solution.py:451
  4.5 0.0 copy-done.2
  4.6 0.0 copy-done.3
  4.6 177.9 %shard_map.59 = (bf16[2,2,128,16384]{3,2,1,0:T(8,128)(2,1)}, bf16[2,2,128,16384]{3,2,1,0:T(8,128)(2,1)}, bf16[2,2,2,72,16384]{4,3,2,1,0:T(8,128)(2,1)}, s32[4,8,128]{2,1,0:T(8,128)S(1)}, f32[512,576]{1,0:T(8,128)S(1)}) custom-call(bf16[128,16384]{1,0:T(8,128)(2,1)} %part_ref.1, bf16[72,16384]{1,0:T(8,128)(2,1)S(1)} %reshape.135.temp_ref, ...), custom_call_target="tpu_custom_call" | custom-call | bytes 356515840 | tf_op jit(solution)/shard_map/pallas_call | solution.py:207
  182.5 0.0 copy-start.1
  182.5 1.0 copy-done.1
  183.6 0.1 multiply_add_fusion
  183.7 0.1 reshape.145
  183.8 1.7 select_reduce_fusion
  185.5 0.6 fusion.both_ref
  186.1 11.0 %shard_map.60 = f32[2,2,2,4,8,128]{5,4,3,2,1,0:T(8,128)} custom-call(f32[4,8,128]{2,1,0:T(8,128)} %fusion.both_ref), custom_call_target="tpu_custom_call" | custom-call | bytes 20000000 | tf_op jit(solution)/shard_map/pallas_call | solution.py:295
  197.1 0.7 dynamic-slice_bitcast_fusion.1
  197.9 0.1 iota.66
  198.0 0.1 iota.64
  198.1 0.1 select_n.90
  198.2 0.1 iota.61
  198.2 0.1 iota.62
  198.3 0.2 select_convert_fusion.mix_ref
  198.5 1.0 slice_convert_fusion
  199.5 0.3 select_reduce_fusion.1
  199.8 0.1 broadcast_in_dim.59.least_ref
  199.9 125.9 %shard_map.61 = f32[18,4,16384]{2,1,0:T(4,128)S(1)} custom-call(bf16[288,1024]{1,0:T(8,128)(2,1)S(1)} %select_convert_fusion.mix_ref, f32[72,128]{1,0:T(8,128)S(1)} %broadcast_in_dim.59.least_ref, bf16[512,16384]{1,0:T(8,128)(2,1)} %bitcast.35, bf16[512,16384]{1,0:T(8,128)(2,1)} %bitcast.36), custom_call_target="tpu_custom_call" | custom-call | flops 9663676416 | bytes 33554432 | tf_op jit(solution)/shard_map/pallas_call | solution.py:411
  325.8 0.0 copy-start
  325.8 2.1 copy-done
  327.9 0.7 dynamic-slice_convert_fusion
  328.6 0.5 slice_bitcast_fusion
  329.1 4.9 %copy.7 = f32[4,18,16384]{2,0,1:T(4,128)} copy(f32[4,18,16384]{2,0,1:T(4,128)} %bitcast.34) | data formatting | bytes 9437184
  (11 shorter events, 0.1 us)
Async XLA Ops:
  0.6 3.9 %copy-start.2 = (s32[128]{0:T(128)S(1)}, s32[128]{0:T(128)}, u32[]{:S(2)}) copy-start(s32[128]{0:T(128)} %param.7) | copy-start | bytes 1540
  0.6 3.9 %copy-start.3 = (s32[128,1]{0,1:T(1,128)S(1)}, s32[128,1]{0,1:T(1,128)}, u32[]{:S(2)}) copy-start(s32[128,1]{0,1:T(1,128)} %param.6) | copy-start | bytes 1540
  182.5 1.1 copy-start.1
  325.8 2.1 copy-start

commit v3 on v2

--- a/solution.py
+++ b/solution.py
@@ -397,8 +397,16 @@
             send_h(j, k).wait_send()
         return carry
 
-    for stage in (form, merge, finish, drain):
-        lax.fori_loop(0, steps, stage, 0)
+    def turn(t, carry):
+        for stage, late in ((form, 0), (merge, 3), (finish, 6)):
+            @pl.when((t >= late) & (t < steps + late))
+            def _(stage=stage, late=late):
+                stage(t - late, 0)
+
+        return carry
+
+    lax.fori_loop(0, steps + 6, turn, 0)
+    lax.fori_loop(0, steps, drain, 0)
 
 
 def sum_blocks(n, rots, mix, least, parts, sibs):

time: 335 us -> 324 us (0.967)
  Pallas kernels: 315 us -> 305 us
    pallas_call x1, Pallas kernels: 126 us -> 116 us  [sum_blocks(): pl.pallas_call(functools.partial(sum_kernel, n), out_shape=jax.ShapeDtype...]
where the time goes in v3:
time: 324 us
  Pallas kernels  305 us (94%)
  local copies, waits for them, and re-layouts  14.5 us (4%)
  other arithmetic  3.93 us (1%)
    pallas_call x1, Pallas kernels, gather_blocks(): pl.pallas_call(functools.partial(gather_kernel, n), out_shape=(jax.ShapeD...  178 us
    pallas_call x1, Pallas kernels, sum_blocks(): pl.pallas_call(functools.partial(sum_kernel, n), out_shape=jax.ShapeDtype...  116 us
    pallas_call x1, Pallas kernels, weigh_blocks(): pl.pallas_call(functools.partial(weigh_kernel, n, columns), out_shape=jax...  11 us
    unnamed x9, local copies, waits for them, and re-layouts  8.1 us

profile of v3, /device:TPU:0, one launch (start us, length us, event | category | flops | bytes accessed | tf_op | source)
XLA Modules:
  0.0 324.0 jit_solution(13331435882528497023)
XLA Ops:
  0.6 0.0 copy-start.2
  0.6 0.0 copy-start.3
  0.7 3.9 %reshape.135.temp_ref = bf16[72,16384]{1,0:T(8,128)(2,1)S(1)} reshape(bf16[18,4,16384]{2,1,0:T(4,128)(2,1)} %bitcast.37) | data formatting | bytes 4718592 | tf_op jit(solution)/shard_map/reshape | solution.py:459
  4.5 0.0 copy-done.2
  4.6 0.0 copy-done.3
  4.6 177.9 %shard_map.59 = (bf16[2,2,128,16384]{3,2,1,0:T(8,128)(2,1)}, bf16[2,2,128,16384]{3,2,1,0:T(8,128)(2,1)}, bf16[2,2,2,72,16384]{4,3,2,1,0:T(8,128)(2,1)}, s32[4,8,128]{2,1,0:T(8,128)S(1)}, f32[512,576]{1,0:T(8,128)S(1)}) custom-call(bf16[128,16384]{1,0:T(8,128)(2,1)} %part_ref.1, bf16[72,16384]{1,0:T(8,128)(2,1)S(1)} %reshape.135.temp_ref, ...), custom_call_target="tpu_custom_call" | custom-call | bytes 356515840 | tf_op jit(solution)/shard_map/pallas_call | solution.py:207
  182.5 0.0 copy-start.1
  182.5 1.0 copy-done.1
  183.6 0.1 multiply_add_fusion
  183.7 0.1 reshape.145
  183.8 1.7 select_reduce_fusion
  185.5 0.6 fusion.both_ref
  186.1 11.0 %shard_map.60 = f32[2,2,2,4,8,128]{5,4,3,2,1,0:T(8,128)} custom-call(f32[4,8,128]{2,1,0:T(8,128)} %fusion.both_ref), custom_call_target="tpu_custom_call" | custom-call | bytes 20000000 | tf_op jit(solution)/shard_map/pallas_call | solution.py:295
  197.1 0.7 dynamic-slice_bitcast_fusion.1
  197.9 0.1 iota.66
  198.0 0.1 iota.64
  198.1 0.1 select_n.90
  198.2 0.1 iota.61
  198.2 0.1 iota.62
  198.3 0.2 select_convert_fusion.mix_ref
  198.5 1.0 slice_convert_fusion
  199.5 0.3 select_reduce_fusion.1
  199.8 0.1 broadcast_in_dim.59.least_ref
  199.9 115.9 %shard_map.61 = f32[18,4,16384]{2,1,0:T(4,128)S(1)} custom-call(bf16[288,1024]{1,0:T(8,128)(2,1)S(1)} %select_convert_fusion.mix_ref, f32[72,128]{1,0:T(8,128)S(1)} %broadcast_in_dim.59.least_ref, bf16[512,16384]{1,0:T(8,128)(2,1)} %bitcast.35, bf16[512,16384]{1,0:T(8,128)(2,1)} %bitcast.36), custom_call_target="tpu_custom_call" | custom-call | flops 9663676416 | bytes 33554432 | tf_op jit(solution)/shard_map/pallas_call | solution.py:419
  315.8 0.0 copy-start
  315.8 2.1 copy-done
  317.9 0.7 dynamic-slice_convert_fusion
  318.6 0.5 slice_bitcast_fusion
  319.1 4.9 %copy.7 = f32[4,18,16384]{2,0,1:T(4,128)} copy(f32[4,18,16384]{2,0,1:T(4,128)} %bitcast.34) | data formatting | bytes 9437184
  (11 shorter events, 0.1 us)
Async XLA Ops:
  0.6 3.9 %copy-start.2 = (s32[128]{0:T(128)S(1)}, s32[128]{0:T(128)}, u32[]{:S(2)}) copy-start(s32[128]{0:T(128)} %param.7) | copy-start | bytes 1540
  0.6 3.9 %copy-start.3 = (s32[128,1]{0,1:T(1,128)S(1)}, s32[128,1]{0,1:T(1,128)}, u32[]{:S(2)}) copy-start(s32[128,1]{0,1:T(1,128)} %param.6) | copy-start | bytes 1540
  182.5 1.1 copy-start.1
  315.8 2.1 copy-start
